TPU v7x, 128 devices: a whole 4x4x4 slice. The times are simulated.
128 devices in a mesh: tm: 32 (over y, x, core), hid: 4 (over z).
Axes of the slice: x: 4, y: 4, z: 4, core: 2. Of those that a mesh axis runs over, the one named last changes fastest.
Arguments:
- gate_inputs: bfloat16 [8192, 3, 4096], P('tm', None, 'hid'), may hold values from -6 to 16
- recurrent: bfloat16 [3, 4096, 4096], P(None, None, 'hid'), may hold values from -0.09375 to 0.09375
- initial_state: float32 [4096], P('hid'), may hold values from -0.9 to 0.9
- guess: bfloat16 [8192, 4096], P('tm', 'hid'), may hold values from -0.8984375 to 0.8984375
Outputs:
- trajectory: bfloat16 [8192, 4096], P('tm', 'hid')
All inputs are finite; a program needn't handle non-finite values.
Results may differ from a plain program's by a relative error of at most 0.003.
Values may be sent and summed in bfloat16 or wider, within the bound.
A program may use at most 128 MiB of HBM per device.

v0:
```python
import jax
import jax.numpy as jnp
from jax import lax
from jax.sharding import PartitionSpec as P

ITERS = 2


def from_behind(x, axis, by):
    size = lax.axis_size(axis)
    pairs = [(i, i + by) for i in range(size) if 0 <= i + by < size]
    return lax.ppermute(x, axis, pairs)


def prefix(value, axis, join, neutral):
    count, mine = (lax.axis_size(axis), lax.axis_index(axis))
    pieces = jax.tree.map(lambda part: lax.all_gather(part, axis), value)
    total = jax.tree.map(
        lambda part, zero: jnp.full_like(part, 0) + jnp.asarray(zero, part.dtype), value, neutral
    )

    def turn(position, total):
        longer = join(total, jax.tree.map(lambda part: part[position], pieces))
        return jax.tree.map(lambda new, old: jnp.where(position < mine, new, old), longer, total)

    return lax.fori_loop(0, count - 1, turn, total)


def compose(earlier, later):
    earlier_gain, earlier_shift = earlier
    later_gain, later_shift = later
    return (later_gain * earlier_gain, later_gain * earlier_shift + later_shift)


def boundary_row(states):
    return from_behind(states[-1], "tm", 1)


def per_device(gate_inputs, recurrent, initial_state, guess):
    rows = gate_inputs.shape[0]
    own = recurrent.shape[2]
    hid_index = lax.axis_index("hid")
    time_index = lax.axis_index("tm")
    own_block = lax.dynamic_slice_in_dim(recurrent, hid_index * own, own, 1)
    diagonal = jnp.diagonal(own_block, axis1=1, axis2=2).astype(jnp.float32)
    inputs = gate_inputs.astype(jnp.float32)
    states = guess.astype(jnp.float32)
    entering = initial_state
    for step in range(ITERS):
        incoming = jnp.where(time_index == 0, initial_state, boundary_row(states))
        previous = jnp.concatenate([incoming[None, :], states[:-1]], axis=0)
        empty = jnp.zeros((rows, 3, own), jnp.float32)
        piece = lax.all_gather(previous.astype(jnp.bfloat16), "hid", axis=1, tiled=True)
        weight_rows = lax.slice_in_dim(recurrent, 0, piece.shape[1], axis=1)
        total = empty + jnp.einsum(
            "tk,gko->tgo", piece, weight_rows, preferred_element_type=jnp.float32
        )
        memory = total[:, 2]
        update = jax.nn.sigmoid(inputs[:, 0] + total[:, 0])
        reset = jax.nn.sigmoid(inputs[:, 1] + total[:, 1])
        candidate = jnp.tanh(inputs[:, 2] + reset * memory)
        target = (1.0 - update) * candidate + update * previous
        slope = (
            update * (1.0 - update) * diagonal[0] * (previous - candidate)
            + (1.0 - update)
            * (1.0 - candidate * candidate)
            * (reset * (1.0 - reset) * diagonal[1] * memory + reset * diagonal[2])
            + update
        )
        offset = target - slope * previous
        gains, shifts = lax.associative_scan(compose, (slope, offset), axis=0)
        identity = (jnp.ones((own,), jnp.float32), jnp.zeros((own,), jnp.float32))
        before_gain, before_shift = prefix((gains[-1], shifts[-1]), "tm", compose, identity)
        entering = before_gain * initial_state + before_shift
        states = gains * entering[None, :] + shifts
    return states.astype(jnp.bfloat16)


def solution(mesh):
    in_specs = (P("tm", None, "hid"), P(None, None, "hid"), P("hid"), P("tm", "hid"))
    out_specs = P("tm", "hid")
    return jax.shard_map(
        per_device, mesh=mesh, in_specs=in_specs, out_specs=out_specs, check_vma=False
    )
```

profile of v0, /device:TPU:25, one launch (start us, length us, event | category | flops | bytes accessed | tf_op | source)
XLA Modules:
  0.0 477.0 jit_solution(14330377499558345989)
XLA Ops:
  7.3 3.7 collective-permute-start
  13.3 6.1 %constant_dynamic-slice_fusion.4 = bf16[3,1024,1024]{2,1,0:T(8,128)(2,1)} fusion(bf16[3,4096,1024]{2,1,0:T(8,128)(2,1)} %param.9, s32[]{:T(128)S(6)} %select_n.77), kind=kLoop, calls=%fused_computation.194 | loop fusion | bytes 12582916 | tf_op jit(solution)/shard_map/dynamic_slice | solution.py:44
  19.4 11.5 %copy.12 = bf16[3,1024,1024]{2,0,1:T(4,128)(2,1)} copy(bf16[3,1024,1024]{2,1,0:T(8,128)(2,1)} %constant_dynamic-slice_fusion.4) | data formatting | bytes 12582912
  32.8 12.7 %gather_fusion = bf16[1024,3]{0,1:T(4,128)(2,1)S(1)} fusion(bf16[3,1024,1024]{2,0,1:T(4,128)(2,1)} %copy.12, s32[1024]{0:T(1024)S(1)} %bitcast.117), kind=kCustom, calls=%fused_computation | custom fusion | bytes 20480 | tf_op jit(solution)/shard_map/jit(diagonal)/gather | solution.py:45
  46.5 12.3 %fusion.2 = f32[256,3,1024]{2,0,1:T(8,128)S(1)} fusion(bf16[3,4096,1024]{2,1,0:T(8,128)(2,1)} %param.9, bf16[256,4096]{1,0:T(8,128)(2,1)} %all-gather.7.cloned.1.call-done), kind=kOutput, calls=%fused_computation.11 | convolution fusion | flops 6442450944 | bytes 30408704 | tf_op jit(solution)/shard_map/tk,gko->tgo/dot_general | solution.py:55
  58.8 2.6 fusion.10
  61.3 3.3 slice.539
  64.6 3.2 slice.540
  67.8 3.2 slice.576
  71.1 3.2 slice.577
  74.3 2.7 fusion.69
  145.9 3.3 slice.538
  149.2 3.3 slice.611
  182.0 2.6 pad.224
  184.6 2.6 pad.225
  189.2 4.6 pad.227
  195.5 2.6 pad.208
  201.9 2.9 add_multiply_fusion.3
  205.7 4.6 pad.226
  211.1 24.7 %all-gather.1 = f32[32,1,1024]{2,1,0:T(1,128)S(1)} all-gather(f32[1,1,1024]{2,1,0:T(1,128)S(1)} %add_bitcast_fusion.2), channel_id=1, replica_groups=mesh['tm'=32,'hid'=4] {'tm'}, dimensions={0}, use_global_device_ids=true | all-gather | bytes 135168 | tf_op jit(solution)/shard_map/all_gather | solution.py:17
  235.8 4.6 pad.211
  242.3 4.7 pad.210
  247.8 23.2 %all-gather = f32[32,1,1024]{2,1,0:T(1,128)S(1)} all-gather(f32[1,1,1024]{2,1,0:T(1,128)S(1)} %add_bitcast_fusion.3), channel_id=1, replica_groups=mesh['tm'=32,'hid'=4] {'tm'}, dimensions={0}, use_global_device_ids=true | all-gather | bytes 135168 | tf_op jit(solution)/shard_map/all_gather | solution.py:17
  272.9 2.6 multiply_add_fusion
  279.6 34.2 %all-gather.9.cloned.1.call-done = bf16[256,4096]{1,0:T(8,128)(2,1)} async-done(((bf16[256,1024]{1,0:T(8,128)(2,1)}), bf16[256,4096]{1,0:T(8,128)(2,1)}) %all-gather.9.cloned.1.call-update) | async-done | bytes 2097168 | tf_op jit(solution)/shard_map/all_gather | solution.py:53
  313.8 12.3 %fusion = f32[256,3,1024]{2,0,1:T(8,128)S(1)} fusion(bf16[3,4096,1024]{2,1,0:T(8,128)(2,1)} %param.9, bf16[256,4096]{1,0:T(8,128)(2,1)} %all-gather.9.cloned.1.call-done), kind=kOutput, calls=%fused_computation.9 | convolution fusion | flops 6442450944 | bytes 30408704 | tf_op jit(solution)/shard_map/tk,gko->tgo/dot_general | solution.py:55
  326.1 2.6 fusion.17
  332.9 3.2 slice.657
  409.3 24.7 %all-gather.3 = f32[32,1,1024]{2,1,0:T(1,128)S(1)} all-gather(f32[1,1,1024]{2,1,0:T(1,128)S(1)} %add_bitcast_fusion), channel_id=1, replica_groups=mesh['tm'=32,'hid'=4] {'tm'}, dimensions={0}, use_global_device_ids=true | all-gather | bytes 135168 | tf_op jit(solution)/shard_map/all_gather | solution.py:17
  438.0 4.6 pad.242
  443.4 22.4 %all-gather.2 = f32[32,1,1024]{2,1,0:T(1,128)S(1)} all-gather(f32[1,1,1024]{2,1,0:T(1,128)S(1)} %add_bitcast_fusion.1), channel_id=1, replica_groups=mesh['tm'=32,'hid'=4] {'tm'}, dimensions={0}, use_global_device_ids=true | all-gather | bytes 135168 | tf_op jit(solution)/shard_map/all_gather | solution.py:17
  467.7 2.5 add_convert_fusion
  (484 shorter events, 206.3 us)
Async XLA Ops:
  6.5 39.9 %all-gather.7.cloned.1.call-start = ((), (), s32[]{:S(2)}) async-start(), calls=%async_computation | async-start | bytes 2621440 | tf_op jit(solution)/shard_map/all_gather | solution.py:53
  7.3 4.9 %collective-permute-start = (f32[1024]{0:T(1024)S(1)}, f32[1024]{0:T(1024)S(1)}, u32[]{:S(2)}, u32[]{:S(2)}) collective-permute-start(f32[1024]{0:T(1024)S(1)} %bitcast.138), channel_id=1, source_target_pairs={{0,4},{4,8},{8,12},{12,16},{16,20},{20,24},{24,28},{28,32},{32,36}... | collective-permute-start | bytes 12296 | tf_op jit(solution)/shard_map/ppermute | solution.py:12
  13.2 300.6 %all-gather.9.cloned.1.call-start = ((), (), s32[]{:S(2)}) async-start(), calls=%async_computation.1 | async-start | bytes 2621440 | tf_op jit(solution)/shard_map/all_gather | solution.py:53
  45.5 13.2 %copy-start.20 = (f32[1,1024]{1,0:T(1,128)}, f32[1,1024]{1,0:T(1,128)S(1)}, u32[]{:S(2)}) copy-start(f32[1,1024]{1,0:T(1,128)S(1)} %get-tuple-element.364) | copy-start | bytes 12292
  45.5 13.2 %copy-start.22 = (f32[1,1024]{1,0:T(1,128)}, f32[1,1024]{1,0:T(1,128)S(1)}, u32[]{:S(2)}) copy-start(f32[1,1024]{1,0:T(1,128)S(1)} %get-tuple-element.365) | copy-start | bytes 12292
  46.5 12.3 %copy-start.3 = (f32[255,1024]{1,0:T(8,128)S(1)}, f32[255,1024]{1,0:T(8,128)}, u32[]{:S(2)}) copy-start(f32[255,1024]{1,0:T(8,128)} %copy-done.2) | copy-start | bytes 3133444
  135.4 19.7 %copy-start.13 = (f32[7,1024]{1,0:T(8,128)S(1)}, f32[7,1024]{1,0:T(8,128)}, u32[]{:S(2)}) copy-start(f32[7,1024]{1,0:T(8,128)} %slice.554) | copy-start | bytes 86020
  135.4 19.7 %copy-start.14 = (f32[7,1024]{1,0:T(8,128)S(1)}, f32[7,1024]{1,0:T(8,128)}, u32[]{:S(2)}) copy-start(f32[7,1024]{1,0:T(8,128)} %slice.603) | copy-start | bytes 86020
  135.4 21.8 %copy-start.10 = (f32[15,1024]{1,0:T(8,128)S(1)}, f32[15,1024]{1,0:T(8,128)}, u32[]{:S(2)}) copy-start(f32[15,1024]{1,0:T(8,128)} %slice.550) | copy-start | bytes 184324
  139.7 14.9 %copy-start.27 = (f32[2,1024]{1,0:T(2,128)S(1)}, f32[2,1024]{1,0:T(2,128)}, u32[]{:S(2)}) copy-start(f32[2,1024]{1,0:T(2,128)} %get-tuple-element.379) | copy-start | bytes 24580
  139.7 14.9 %copy-start.26 = (f32[2,1024]{1,0:T(2,128)S(1)}, f32[2,1024]{1,0:T(2,128)}, u32[]{:S(2)}) copy-start(f32[2,1024]{1,0:T(2,128)} %get-tuple-element.378) | copy-start | bytes 24580
  139.7 15.0 %copy-start.45 = (f32[1,1024]{1,0:T(1,128)S(1)}, f32[1,1024]{1,0:T(1,128)}, u32[]{:S(2)}) copy-start(f32[1,1024]{1,0:T(1,128)} %get-tuple-element.357) | copy-start | bytes 12292
  139.7 15.0 %copy-start.46 = (f32[1,1024]{1,0:T(1,128)S(1)}, f32[1,1024]{1,0:T(1,128)}, u32[]{:S(2)}) copy-start(f32[1,1024]{1,0:T(1,128)} %get-tuple-element.358) | copy-start | bytes 12292
  139.7 15.0 %copy-start.47 = (f32[1,1024]{1,0:T(1,128)S(1)}, f32[1,1024]{1,0:T(1,128)}, u32[]{:S(2)}) copy-start(f32[1,1024]{1,0:T(1,128)} %get-tuple-element.359) | copy-start | bytes 12292
  139.7 15.0 %copy-start.48 = (f32[1,1024]{1,0:T(1,128)S(1)}, f32[1,1024]{1,0:T(1,128)}, u32[]{:S(2)}) copy-start(f32[1,1024]{1,0:T(1,128)} %get-tuple-element.360) | copy-start | bytes 12292
  139.7 15.1 %copy-start.18 = (f32[3,1024]{1,0:T(4,128)S(1)}, f32[3,1024]{1,0:T(4,128)}, u32[]{:S(2)}) copy-start(f32[3,1024]{1,0:T(4,128)} %slice.558) | copy-start | bytes 36868
  139.7 15.1 %copy-start.19 = (f32[3,1024]{1,0:T(4,128)S(1)}, f32[3,1024]{1,0:T(4,128)}, u32[]{:S(2)}) copy-start(f32[3,1024]{1,0:T(4,128)} %slice.601) | copy-start | bytes 36868
  139.7 15.1 %copy-start.40 = (f32[1,1024]{1,0:T(1,128)S(1)}, f32[1,1024]{1,0:T(1,128)}, u32[]{:S(2)}) copy-start(f32[1,1024]{1,0:T(1,128)} %slice.738) | copy-start | bytes 12292
  139.8 15.2 %copy-start.39 = (f32[1,1024]{1,0:T(1,128)S(1)}, f32[1,1024]{1,0:T(1,128)}, u32[]{:S(2)}) copy-start(f32[1,1024]{1,0:T(1,128)} %slice.712) | copy-start | bytes 12292
  181.2 12.6 %copy-start.30 = (f32[1,1024]{1,0:T(1,128)S(1)}, f32[1,1024]{1,0:T(1,128)}, u32[]{:S(2)}) copy-start(f32[1,1024]{1,0:T(1,128)} %slice.708) | copy-start | bytes 12292
  182.0 16.2 %copy-start.6 = (f32[64,1024]{1,0:T(8,128)S(1)}, f32[64,1024]{1,0:T(8,128)}, u32[]{:S(2)}) copy-start(f32[64,1024]{1,0:T(8,128)} %add.477) | copy-start | bytes 786436
  204.8 35.6 %copy-start.28 = (f32[1,1024]{1,0:T(1,128)S(1)}, f32[1,1024]{1,0:T(1,128)}, u32[]{:S(2)}) copy-start(f32[1,1024]{1,0:T(1,128)} %slice.707) | copy-start | bytes 12292
  205.7 67.2 %copy-start.17 = (f32[1024]{0:T(1024)S(1)}, f32[1024]{0:T(1024)}, u32[]{:S(2)}) copy-start(f32[1024]{0:T(1024)} %param.10) | copy-start | bytes 12292
  275.6 3.1 collective-permute-start.1
  279.6 46.5 %copy-start.21 = (f32[1,1024]{1,0:T(1,128)S(1)}, f32[1,1024]{1,0:T(1,128)}, u32[]{:S(2)}) copy-start(f32[1,1024]{1,0:T(1,128)} %copy-done.20) | copy-start | bytes 12292
  279.6 46.5 %copy-start.23 = (f32[1,1024]{1,0:T(1,128)S(1)}, f32[1,1024]{1,0:T(1,128)}, u32[]{:S(2)}) copy-start(f32[1,1024]{1,0:T(1,128)} %copy-done.22) | copy-start | bytes 12292
  313.8 12.3 %copy-start.1 = (f32[256,1024]{1,0:T(8,128)S(1)}, f32[256,1024]{1,0:T(8,128)}, u32[]{:S(2)}) copy-start(f32[256,1024]{1,0:T(8,128)} %copy-done) | copy-start | bytes 3145732
  340.4 56.8 %copy-start.4 = (f32[256,1024]{1,0:T(8,128)S(1)}, f32[256,1024]{1,0:T(8,128)}, u32[]{:S(2)}) copy-start(f32[256,1024]{1,0:T(8,128)} %get-tuple-element.296) | copy-start | bytes 3145732
  394.3 9.0 %copy-start.15 = (f32[7,1024]{1,0:T(8,128)S(1)}, f32[7,1024]{1,0:T(8,128)}, u32[]{:S(2)}) copy-start(f32[7,1024]{1,0:T(8,128)} %slice.635) | copy-start | bytes 86020
  394.3 9.0 %copy-start.16 = (f32[7,1024]{1,0:T(8,128)S(1)}, f32[7,1024]{1,0:T(8,128)}, u32[]{:S(2)}) copy-start(f32[7,1024]{1,0:T(8,128)} %slice.684) | copy-start | bytes 86020
  394.3 9.2 %copy-start.11 = (f32[15,1024]{1,0:T(8,128)S(1)}, f32[15,1024]{1,0:T(8,128)}, u32[]{:S(2)}) copy-start(f32[15,1024]{1,0:T(8,128)} %slice.631) | copy-start | bytes 184324
  394.3 9.2 %copy-start.12 = (f32[15,1024]{1,0:T(8,128)S(1)}, f32[15,1024]{1,0:T(8,128)}, u32[]{:S(2)}) copy-start(f32[15,1024]{1,0:T(8,128)} %slice.686) | copy-start | bytes 184324
  (21 other events, 105.8 us)
Sparse Core Ops, SparseCore 0:
  13.4 33.0 all-gather.6
  279.7 34.0 all-gather.8
where the time goes:
time: 487 us; the launch traced here: 477 us
  local copies, waits for them, and re-layouts  219 us (45%)
  blocking collectives  95 us (20%)
  other arithmetic  79.8 us (16%)
  waiting for transfers between devices  36 us (7%)
  matrix products  24.5 us (5%)
  between operations  14.8 us (3%)
  starting transfers between devices  5.97 us (1%)
    slice x104, local copies, waits for them, and re-layouts, per_device(): gains, shifts = lax.associative_scan(compose, (slope, offset), axis=0)  140 us
    all_gather x4, blocking collectives, prefix(): pieces = jax.tree.map(lambda part: lax.all_gather(part, axis), value)  95 us
    pad x56, local copies, waits for them, and re-layouts, per_device(): gains, shifts = lax.associative_scan(compose, (slope, offset), axis=0)  45.2 us
    all_gather x2, waiting for transfers between devices, per_device(): lax.all_gather(previous.astype(jnp.bfloat16), 'hid', axis=1, tiled=True)  35.1 us
    mul x26, other arithmetic, compose(): return (later_gain * earlier_gain, later_gain * earlier_shift + later_shift)  32.1 us
    dot_general x2, matrix products, per_device(): jnp.einsum('tk,gko->tgo', piece, weight_rows, preferred_element_type=jnp....  24.5 us
    concatenate x27, other arithmetic, per_device(): gains, shifts = lax.associative_scan(compose, (slope, offset), axis=0)  14.6 us
    add x27, other arithmetic, per_device(): gains, shifts = lax.associative_scan(compose, (slope, offset), axis=0)  13.4 us
  transfers between devices with their start and end apart: 4, of which 3 were waited for; matrix products, arithmetic and copies ran while one was open for 7% of the time, Pallas kernels for 0%

commit v1 on v0

v1 whole, which is shorter than its diff:
```python
import functools

import jax
import jax.numpy as jnp
from jax import lax
from jax.experimental import pallas as pl
from jax.experimental.pallas import tpu as pltpu
from jax.sharding import PartitionSpec as P

ITERS = 2
ROWS = 256
UNITS = 1024
SUB = 16
CW = 256
NC = UNITS // CW
GROUP = 8
LINES = 4
MESH = pl.DeviceIdType.MESH


def dot(a, b):
    return jnp.dot(a, b, preferred_element_type=jnp.float32)


def sigmoid(x):
    return 0.5 * jnp.tanh(0.5 * x) + 0.5


def kernel(
    gi, w, h0, guess, out,
    wv, giv, gv, xb, acc, ip, hprev, gs, ss, eg, es, diag, bnd, tot1, tot2, got1, got2, perm, states, outv,
    load_sem, w_sem, out_sem, bnd_sem, right_s, left_s, fwd_s, z_r, edge_s, edge_r, s1, r1, s2, r2,
):
    tm = lax.axis_index("tm")
    z = lax.axis_index("hid")
    y, q = tm // GROUP, lax.rem(tm, GROUP)
    right, left = lax.rem(z + 1, 4), lax.rem(z + 3, 4)

    load_guess = pltpu.make_async_copy(guess, gv, load_sem.at[0])
    load_inputs = pltpu.make_async_copy(gi, giv, load_sem.at[1])

    def load_weights(d):
        rows = pl.ds(pl.multiple_of(lax.rem(z + d, 4) * UNITS, UNITS), UNITS)
        return pltpu.make_async_copy(w.at[:, rows, :], wv.at[d], w_sem.at[d])

    load_guess.start()
    load_weights(0).start()
    load_inputs.start()
    for d in (1, 3, 2):
        load_weights(d).start()

    barrier = pltpu.get_barrier_semaphore()

    def greet(device):
        pl.semaphore_signal(barrier, inc=1, device_id=device, device_id_type=MESH)

    greet((tm, right))
    greet((tm, left))
    greet((lax.rem(tm + 1, 32), z))
    greet((lax.rem(tm + 31, 32), z))
    for j in range(1, GROUP):
        greet((y * GROUP + lax.rem(q + j, GROUP), z))
    for j in range(1, LINES):
        greet((lax.rem(y + j, LINES) * GROUP + q, z))

    r = lax.broadcasted_iota(jnp.int32, (ROWS, ROWS), 0)
    t = lax.broadcasted_iota(jnp.int32, (ROWS, ROWS), 1)
    time = (r & (SUB - 1)) * SUB + (r >> 4)
    perm[0] = jnp.where(t == time, 1.0, 0.0).astype(jnp.bfloat16)
    perm[1] = jnp.where(t == time - 1, 1.0, 0.0).astype(jnp.bfloat16)

    load_guess.wait()

    def shift(n, carry):
        cols = pl.ds(pl.multiple_of(n * CW, CW), CW)
        rows = dot(perm[1], gv[:, cols])
        hprev[n] = rows
        xb[0, 0, n] = rows.astype(jnp.bfloat16)
        return carry

    lax.fori_loop(0, NC, shift, 0)

    pl.semaphore_wait(barrier, 4 + (GROUP - 1) + (LINES - 1))

    def remote(src, dst, send, recv, device):
        return pltpu.make_async_remote_copy(
            src_ref=src, dst_ref=dst, send_sem=send, recv_sem=recv, device_id=device, device_id_type=MESH
        )

    def part(it, d, c):
        return xb.at[it, d, c, pl.ds(SUB, ROWS - SUB), :] if it == 0 else xb.at[it, d, c]

    def to_right(it, c):
        return remote(part(it, 0, c), part(it, 3, c), right_s.at[it, c], z_r.at[it, 3, c], (tm, right))

    def to_left(it, c):
        return remote(part(it, 0, c), part(it, 1, c), left_s.at[it, c], z_r.at[it, 1, c], (tm, left))

    def forward(it, c):
        src, device = (3, right) if c < NC // 2 else (1, left)
        return remote(part(it, src, c), part(it, 2, c), fwd_s.at[it, c], z_r.at[it, 2, c], (tm, device))

    def edge(d, lo, hi):
        return xb.at[0, d, pl.ds(lo, hi - lo), pl.ds(0, SUB), :]

    half = NC // 2
    edges = (
        remote(edge(0, 0, NC), edge(3, 0, NC), edge_s.at[0], edge_r.at[0], (tm, right)),
        remote(edge(0, 0, NC), edge(1, 0, NC), edge_s.at[1], edge_r.at[1], (tm, left)),
        remote(edge(3, 0, half), edge(2, 0, half), edge_s.at[2], edge_r.at[2], (tm, right)),
        remote(edge(1, half, NC), edge(2, half, NC), edge_s.at[3], edge_r.at[3], (tm, left)),
    )

    boundary = remote(
        guess.at[pl.ds(ROWS - SUB, SUB), :], bnd, bnd_sem.at[0], bnd_sem.at[1], (lax.rem(tm + 1, 32), z)
    )
    boundary.start()
    for c in range(half):
        to_right(0, c).start()
        to_left(0, half + c).start()
    boundary.wait_recv()
    first = lax.broadcasted_iota(jnp.int32, (SUB, CW), 0) == 0
    for n in range(NC):
        cols = slice(n * CW, (n + 1) * CW)
        row = jnp.where(tm == 0, h0[:, cols], bnd[SUB - 1 :, cols].astype(jnp.float32))
        tile = jnp.where(first, row, hprev[n, 0:SUB, :])
        hprev[n, 0:SUB, :] = tile
        xb[0, 0, n, 0:SUB, :] = tile.astype(jnp.bfloat16)
    edges[0].start()
    edges[1].start()
    for c in range(half):
        to_right(0, half + c).start()
        to_left(0, c).start()

    load_inputs.wait()

    def order_inputs(n, carry):
        cols = pl.ds(pl.multiple_of(n * CW, CW), CW)
        for g in range(3):
            ip[n, g] = dot(perm[0], giv[g, :, cols])
        return carry

    lax.fori_loop(0, NC, order_inputs, 0)

    def accumulate(it, pairs, start):
        def body(n, carry):
            cols = pl.ds(pl.multiple_of(n * CW, CW), CW)
            for g in range(3):
                total = None
                for d, c in pairs:
                    term = dot(xb[it, d, c], wv[d, g, c * CW : (c + 1) * CW, cols])
                    total = term if total is None else total + term
                acc[n, g] = total if start else acc[n, g] + total
            return carry

        lax.fori_loop(0, NC, body, 0)

    sub_row = lax.broadcasted_iota(jnp.int32, (SUB, CW), 0)

    def tile_of(i):
        return slice(i * SUB, (i + 1) * SUB)

    def stage1(it, n, j):
        device = (y * GROUP + lax.rem(q + j, GROUP), z)
        return remote(tot1.at[it, n], got1.at[it, n, q], s1.at[it, n, j], r1.at[it, n, q], device)

    def stage2(it, n, j):
        device = (lax.rem(y + j, LINES) * GROUP + q, z)
        return remote(tot2.at[it, n], got2.at[it, n, y], s2.at[it, n, j], r2.at[it, n, y], device)

    def gates(it, n):
        d0, d1, d2 = (jnp.broadcast_to(diag[n, g : g + 1, :], (SUB, CW)) for g in range(3))
        gain = shift_ = None
        for i in range(ROWS // SUB):
            rows = tile_of(i)
            previous = hprev[n, rows, :]
            memory = acc[n, 2, rows, :]
            update = sigmoid(ip[n, 0, rows, :] + acc[n, 0, rows, :])
            reset = sigmoid(ip[n, 1, rows, :] + acc[n, 1, rows, :])
            candidate = jnp.tanh(ip[n, 2, rows, :] + reset * memory)
            keep = 1.0 - update
            gap = previous - candidate
            target = candidate + update * gap
            slope = update + keep * (
                update * gap * d0
                + (1.0 - candidate * candidate) * reset * ((1.0 - reset) * memory * d1 + d2)
            )
            offset = target - slope * previous
            gain = slope if gain is None else slope * gain
            shift_ = offset if shift_ is None else slope * shift_ + offset
            gs[n, rows, :] = gain
            ss[n, rows, :] = shift_
        for k in (1, 2, 4, 8):
            before_gain = jnp.where(sub_row < k, 1.0, pltpu.roll(gain, k, 0))
            before_shift = jnp.where(sub_row < k, 0.0, pltpu.roll(shift_, k, 0))
            shift_ = gain * before_shift + shift_
            gain = gain * before_gain
        eg[n] = jnp.where(sub_row < 1, 1.0, pltpu.roll(gain, 1, 0))
        es[n] = jnp.where(sub_row < 1, 0.0, pltpu.roll(shift_, 1, 0))
        tot1[it, n, 0:1, :] = gain[SUB - 1 :, :]
        tot1[it, n, 1:2, :] = shift_[SUB - 1 :, :]
        got1[it, n, q, 0:1, :] = gain[SUB - 1 :, :]
        got1[it, n, q, 1:2, :] = shift_[SUB - 1 :, :]

        def send(j, carry):
            stage1(it, n, j).start()
            return carry

        lax.fori_loop(1, GROUP, send, 0)

    def middle(it, n):
        def receive(j, carry):
            source = lax.rem(q + j, GROUP)
            remote(tot1.at[it, n], got1.at[it, n, source], s1.at[it, n, j], r1.at[it, n, source], (tm, z)).wait_recv()
            return carry

        lax.fori_loop(1, GROUP, receive, 0)
        all_gain = jnp.ones((1, CW), jnp.float32)
        all_shift = jnp.zeros((1, CW), jnp.float32)
        my_gain, my_shift = all_gain, all_shift
        for p in range(GROUP):
            g, s = got1[it, n, p, 0:1, :], got1[it, n, p, 1:2, :]
            all_shift = g * all_shift + s
            all_gain = g * all_gain
            my_gain = jnp.where(p < q, all_gain, my_gain)
            my_shift = jnp.where(p < q, all_shift, my_shift)
        tot1_n = n
        tot2[it, n, 0:1, :] = all_gain
        tot2[it, n, 1:2, :] = all_shift
        got2[it, n, y, 0:1, :] = all_gain
        got2[it, n, y, 1:2, :] = all_shift
        bnd_gain_shift[n, 0:1, :] = my_gain
        bnd_gain_shift[n, 1:2, :] = my_shift

        def send(j, carry):
            stage2(it, n, j).start()
            return carry

        lax.fori_loop(1, LINES, send, 0)

    bnd_gain_shift = diag.at[:, 3:5, :]

    def entering_state(it, n):
        def receive(j, carry):
            source = lax.rem(y + j, LINES)
            remote(tot2.at[it, n], got2.at[it, n, source], s2.at[it, n, j], r2.at[it, n, source], (tm, z)).wait_recv()
            return carry

        lax.fori_loop(1, LINES, receive, 0)
        state = h0[:, pl.ds(pl.multiple_of(n * CW, CW), CW)]
        for p in range(LINES - 1):
            g, s = got2[it, n, p, 0:1, :], got2[it, n, p, 1:2, :]
            state = jnp.where(p < y, g * state + s, state)
        state = diag[n, 3:4, :] * state + diag[n, 4:5, :]
        return eg[n] * state + es[n]

    def loop(body):
        def step(n, carry):
            body(n)
            return carry

        lax.fori_loop(0, NC, step, 0)

    def apply_middle(n):
        enter = entering_state(0, n)
        hprev[n, 0:SUB, :] = enter
        xb[1, 0, n, 0:SUB, :] = enter.astype(jnp.bfloat16)
        for i in range(ROWS // SUB - 1):
            state = gs[n, tile_of(i), :] * enter + ss[n, tile_of(i), :]
            hprev[n, tile_of(i + 1), :] = state
            xb[1, 0, n, tile_of(i + 1), :] = state.astype(jnp.bfloat16)
        to_right(1, n).start()
        to_left(1, n).start()

    def store_out(n):
        cols = pl.ds(pl.multiple_of(n * CW, CW), CW)
        return pltpu.make_async_copy(outv.at[n], out.at[:, cols], out_sem.at[n])

    def apply_last(n):
        enter = entering_state(1, n)
        for i in range(ROWS // SUB):
            state = gs[n, tile_of(i), :] * enter + ss[n, tile_of(i), :]
            states[n, tile_of(i), :] = state.astype(jnp.bfloat16)
        outv[n] = dot(perm[0], states[n]).astype(jnp.bfloat16)
        store_out(n).start()

    for it in range(ITERS):
        if it == 0:
            load_weights(0).wait()
            same = r == t
            for n in range(NC):
                block = slice(n * CW, (n + 1) * CW)
                for g in range(3):
                    square = wv[0, g, block, block].astype(jnp.float32)
                    diag[n, g : g + 1, :] = jnp.sum(jnp.where(same, square, 0.0), axis=0, keepdims=True)
        accumulate(it, [(0, c) for c in range(NC)], True)
        for c in range(NC):
            if it == 0 and c == 0:
                load_weights(1).wait()
                load_weights(3).wait()
                edges[0].wait_recv()
                edges[2].start()
                edges[1].wait_recv()
                edges[3].start()
            left_c = (c + half) % NC
            to_right(it, c).wait_recv()
            to_left(it, left_c).wait_recv()
            if c < half:
                forward(it, c).start()
                forward(it, left_c).start()
            accumulate(it, [(3, c), (1, left_c)], False)
        if it == 0:
            load_weights(2).wait()
            edges[2].wait_recv()
            edges[3].wait_recv()
        for c in range(half):
            forward(it, c).wait_recv()
            forward(it, c + half).wait_recv()
            accumulate(it, [(2, c), (2, c + half)], False)
        loop(functools.partial(gates, it))
        loop(functools.partial(middle, it))
        loop(apply_middle if it == 0 else apply_last)

    boundary.wait_send()
    for copy in edges:
        copy.wait_send()
    for it in range(ITERS):
        for c in range(NC):
            to_right(it, c).wait_send()
            to_left(it, c).wait_send()
            forward(it, c).wait_send()

        def drain(n):
            def one(j, carry):
                stage1(it, n, j).wait_send()
                return carry

            def two(j, carry):
                stage2(it, n, j).wait_send()
                return carry

            lax.fori_loop(1, GROUP, one, 0)
            lax.fori_loop(1, LINES, two, 0)

        loop(drain)
    loop(lambda n: store_out(n).wait())


def per_device(gate_inputs, recurrent, initial_state, guess):
    bf16, f32 = jnp.bfloat16, jnp.float32
    dma = pltpu.SemaphoreType.DMA
    hbm = pl.BlockSpec(memory_space=pl.ANY)
    vmem = pl.BlockSpec(memory_space=pltpu.VMEM)
    return pl.pallas_call(
        kernel,
        out_shape=jax.ShapeDtypeStruct((ROWS, UNITS), bf16),
        in_specs=[hbm, hbm, vmem, hbm],
        out_specs=hbm,
        scratch_shapes=[
            pltpu.VMEM((4, 3, UNITS, UNITS), bf16),
            pltpu.VMEM((3, ROWS, UNITS), bf16),
            pltpu.VMEM((ROWS, UNITS), bf16),
            pltpu.VMEM((ITERS, 4, NC, ROWS, CW), bf16),
            pltpu.VMEM((NC, 3, ROWS, CW), f32),
            pltpu.VMEM((NC, 3, ROWS, CW), f32),
            pltpu.VMEM((NC, ROWS, CW), f32),
            pltpu.VMEM((NC, ROWS, CW), f32),
            pltpu.VMEM((NC, ROWS, CW), f32),
            pltpu.VMEM((NC, SUB, CW), f32),
            pltpu.VMEM((NC, SUB, CW), f32),
            pltpu.VMEM((NC, 8, CW), f32),
            pltpu.VMEM((SUB, UNITS), bf16),
            pltpu.VMEM((ITERS, NC, 2, CW), f32),
            pltpu.VMEM((ITERS, NC, 2, CW), f32),
            pltpu.VMEM((ITERS, NC, GROUP, 2, CW), f32),
            pltpu.VMEM((ITERS, NC, LINES, 2, CW), f32),
            pltpu.VMEM((2, ROWS, ROWS), bf16),
            pltpu.VMEM((NC, ROWS, CW), bf16),
            pltpu.VMEM((NC, ROWS, CW), bf16),
            dma((2,)),
            dma((4,)),
            dma((NC,)),
            dma((2,)),
            dma((ITERS, NC)),
            dma((ITERS, NC)),
            dma((ITERS, NC)),
            dma((ITERS, 4, NC)),
            dma((4,)),
            dma((4,)),
            dma((ITERS, NC, GROUP)),
            dma((ITERS, NC, GROUP)),
            dma((ITERS, NC, LINES)),
            dma((ITERS, NC, LINES)),
        ],
        compiler_params=pltpu.CompilerParams(
            collective_id=0, has_side_effects=True, vmem_limit_bytes=58 * 2**20
        ),
    )(jnp.transpose(gate_inputs, (1, 0, 2)), recurrent, initial_state[None, :], guess)


def solution(mesh):
    in_specs = (P("tm", None, "hid"), P(None, None, "hid"), P("hid"), P("tm", "hid"))
    return jax.shard_map(
        per_device, mesh=mesh, in_specs=in_specs, out_specs=P("tm", "hid"), check_vma=False
    )
```

time: 487 us -> 69.8 us (0.14)
  the two profiles are of different devices: /device:TPU:25 before, /device:TPU:1 now
where the time goes in v1:
time: 69.8 us; the launch traced here: 69.6 us
  Pallas kernels  67.7 us (97%)
  local copies, waits for them, and re-layouts  1.87 us (3%)
    pallas_call x1, Pallas kernels, per_device(): pl.pallas_call(kernel, out_shape=jax.ShapeDtypeStruct((ROWS, UNITS), bf16...  67.7 us
    unnamed x1, local copies, waits for them, and re-layouts  1.87 us

profile of v1, /device:TPU:1, one launch (start us, length us, event | category | flops | bytes accessed | tf_op | source)
XLA Modules:
  0.0 69.6 jit_solution(1783114781631550095)
XLA Ops:
  0.0 67.7 %shard_map.46 = bf16[256,1024]{1,0:T(8,128)(2,1)} custom-call(bf16[3,256,1024]{2,1,0:T(8,128)(2,1)} %bitcast.2, bf16[3,4096,1024]{2,1,0:T(8,128)(2,1)} %w.1, f32[1,1024]{1,0:T(1,128)} %bitcast.3, bf16[256,1024]{1,0:T(8,128)(2,1)} %guess.1), custom_call_target="tpu_custom_call" | custom-call | tf_op jit(solution)/shard_map/pallas_call | solution.py:354
  67.7 1.9 %copy.6 = bf16[256,1024]{1,0:T(8,128)(2,1)} copy(bf16[256,1024]{1,0:T(8,128)(2,1)} %shard_map.46) | data formatting | bytes 1048576

commit v2 on v1

--- a/solution.py
+++ b/solution.py
@@ -15,6 +15,13 @@
 NC = UNITS // CW
 GROUP = 8
 LINES = 4
+EARLY = 2
+XS = 4
+STEPS = GROUP * LINES
+AWAY = sorted(
+    [(a, b, c) for a in range(LINES) for b in range(XS) for c in range(2) if (a, b, c) != (0, 0, 0)],
+    key=lambda k: -(min(k[0], LINES - k[0]) + min(k[1], XS - k[1])),
+)
 MESH = pl.DeviceIdType.MESH
 
 
@@ -28,8 +35,8 @@
 
 def kernel(
     gi, w, h0, guess, out,
-    wv, giv, gv, xb, acc, ip, hprev, gs, ss, eg, es, diag, bnd, tot1, tot2, got1, got2, perm, states, outv,
-    load_sem, w_sem, out_sem, bnd_sem, right_s, left_s, fwd_s, z_r, edge_s, edge_r, s1, r1, s2, r2,
+    wv, giv, gv, xb, acc, ip, hprev, gs, ss, eg, es, diag, bnd, total, totals, mine, perm, states, outv,
+    load_sem, w_sem, out_sem, bnd_sem, right_s, left_s, fwd_s, z_r, edge_s, edge_r, t_s, t_r, known,
 ):
     tm = lax.axis_index("tm")
     z = lax.axis_index("hid")
@@ -54,14 +61,19 @@
     def greet(device):
         pl.semaphore_signal(barrier, inc=1, device_id=device, device_id_type=MESH)
 
-    greet((tm, right))
-    greet((tm, left))
-    greet((lax.rem(tm + 1, 32), z))
-    greet((lax.rem(tm + 31, 32), z))
-    for j in range(1, GROUP):
-        greet((y * GROUP + lax.rem(q + j, GROUP), z))
-    for j in range(1, LINES):
-        greet((lax.rem(y + j, LINES) * GROUP + q, z))
+    x, core = q // 2, lax.rem(q, 2)
+
+    def device_at(a, b, c):
+        return lax.rem(y + a, LINES) * GROUP + lax.rem(x + b, XS) * 2 + lax.rem(core + c, 2)
+
+    x_pair = ((device_at(0, 1, 0), z), (device_at(0, XS - 1, 0), z))
+    y_pair = ((device_at(1, 0, 0), z), (device_at(LINES - 1, 0, 0), z))
+    partner = ((device_at(0, 0, 1), z),)
+    later = (lax.rem(tm + 1, STEPS), z)
+    earlier = (lax.rem(tm + STEPS - 1, STEPS), z)
+    near = ((tm, right), (tm, left), later, earlier) + x_pair + y_pair + partner
+    for device in near:
+        greet(device)
 
     r = lax.broadcasted_iota(jnp.int32, (ROWS, ROWS), 0)
     t = lax.broadcasted_iota(jnp.int32, (ROWS, ROWS), 1)
@@ -80,7 +92,7 @@
 
     lax.fori_loop(0, NC, shift, 0)
 
-    pl.semaphore_wait(barrier, 4 + (GROUP - 1) + (LINES - 1))
+    pl.semaphore_wait(barrier, len(near))
 
     def remote(src, dst, send, recv, device):
         return pltpu.make_async_remote_copy(
@@ -112,12 +124,21 @@
     )
 
     boundary = remote(
-        guess.at[pl.ds(ROWS - SUB, SUB), :], bnd, bnd_sem.at[0], bnd_sem.at[1], (lax.rem(tm + 1, 32), z)
+        gv.at[pl.ds(ROWS - SUB, SUB), :], bnd, bnd_sem.at[0], bnd_sem.at[1], later
     )
     boundary.start()
-    for c in range(half):
+    for c in range(EARLY):
         to_right(0, c).start()
-        to_left(0, half + c).start()
+        to_left(0, (half + c) % NC).start()
+
+    def tell(k, devices):
+        for device in devices:
+            pl.semaphore_signal(known.at[k], inc=1, device_id=device, device_id_type=MESH)
+
+    def hear(k, devices):
+        pl.semaphore_wait(known.at[k], len(devices))
+
+    tell(0, x_pair)
     boundary.wait_recv()
     first = lax.broadcasted_iota(jnp.int32, (SUB, CW), 0) == 0
     for n in range(NC):
@@ -128,45 +149,40 @@
         xb[0, 0, n, 0:SUB, :] = tile.astype(jnp.bfloat16)
     edges[0].start()
     edges[1].start()
-    for c in range(half):
-        to_right(0, half + c).start()
-        to_left(0, c).start()
+    for c in range(EARLY, NC):
+        to_right(0, c).start()
+        to_left(0, (half + c) % NC).start()
+    hear(0, x_pair)
+    tell(1, partner)
 
     load_inputs.wait()
 
-    def order_inputs(n, carry):
-        cols = pl.ds(pl.multiple_of(n * CW, CW), CW)
+    for n in range(NC):
         for g in range(3):
-            ip[n, g] = dot(perm[0], giv[g, :, cols])
-        return carry
-
-    lax.fori_loop(0, NC, order_inputs, 0)
-
-    def accumulate(it, pairs, start):
-        def body(n, carry):
-            cols = pl.ds(pl.multiple_of(n * CW, CW), CW)
+            ip[n, g] = dot(perm[0], giv[g, :, n * CW : (n + 1) * CW])
+
+    def accumulate(it, pairs, start=False, parts=range(NC)):
+        for n in parts:
+            cols = slice(n * CW, (n + 1) * CW)
             for g in range(3):
-                total = None
+                terms = None if start else acc[n, g]
                 for d, c in pairs:
                     term = dot(xb[it, d, c], wv[d, g, c * CW : (c + 1) * CW, cols])
-                    total = term if total is None else total + term
-                acc[n, g] = total if start else acc[n, g] + total
-            return carry
-
-        lax.fori_loop(0, NC, body, 0)
+                    terms = term if terms is None else terms + term
+                acc[n, g] = terms
 
     sub_row = lax.broadcasted_iota(jnp.int32, (SUB, CW), 0)
 
     def tile_of(i):
         return slice(i * SUB, (i + 1) * SUB)
 
-    def stage1(it, n, j):
-        device = (y * GROUP + lax.rem(q + j, GROUP), z)
-        return remote(tot1.at[it, n], got1.at[it, n, q], s1.at[it, n, j], r1.at[it, n, q], device)
-
-    def stage2(it, n, j):
-        device = (lax.rem(y + j, LINES) * GROUP + q, z)
-        return remote(tot2.at[it, n], got2.at[it, n, y], s2.at[it, n, j], r2.at[it, n, y], device)
+    def total_to(it, away):
+        device = device_at(*away)
+        copy = remote(total.at[it], totals.at[it, tm], t_s.at[it, device], t_r.at[it, tm], (device, z))
+        return device, copy
+
+    def total_from(it, p):
+        return remote(total.at[it], totals.at[it, p], t_s.at[it, p], t_r.at[it, p], (tm, right))
 
     def gates(it, n):
         d0, d1, d2 = (jnp.broadcast_to(diag[n, g : g + 1, :], (SUB, CW)) for g in range(3))
@@ -197,72 +213,41 @@
             gain = gain * before_gain
         eg[n] = jnp.where(sub_row < 1, 1.0, pltpu.roll(gain, 1, 0))
         es[n] = jnp.where(sub_row < 1, 0.0, pltpu.roll(shift_, 1, 0))
-        tot1[it, n, 0:1, :] = gain[SUB - 1 :, :]
-        tot1[it, n, 1:2, :] = shift_[SUB - 1 :, :]
-        got1[it, n, q, 0:1, :] = gain[SUB - 1 :, :]
-        got1[it, n, q, 1:2, :] = shift_[SUB - 1 :, :]
-
-        def send(j, carry):
-            stage1(it, n, j).start()
+        own = slice(n * CW, (n + 1) * CW)
+        total[it, 0:1, own] = gain[SUB - 1 :, :]
+        total[it, 1:2, own] = shift_[SUB - 1 :, :]
+
+    def send_totals(it):
+        for away in AWAY:
+            device, copy = total_to(it, away)
+
+            @pl.when(device > tm)
+            def _():
+                copy.start()
+
+    def enter_block(it):
+        def receive(p, carry):
+            total_from(it, p).wait_recv()
             return carry
 
-        lax.fori_loop(1, GROUP, send, 0)
-
-    def middle(it, n):
-        def receive(j, carry):
-            source = lax.rem(q + j, GROUP)
-            remote(tot1.at[it, n], got1.at[it, n, source], s1.at[it, n, j], r1.at[it, n, source], (tm, z)).wait_recv()
-            return carry
-
-        lax.fori_loop(1, GROUP, receive, 0)
-        all_gain = jnp.ones((1, CW), jnp.float32)
-        all_shift = jnp.zeros((1, CW), jnp.float32)
-        my_gain, my_shift = all_gain, all_shift
-        for p in range(GROUP):
-            g, s = got1[it, n, p, 0:1, :], got1[it, n, p, 1:2, :]
-            all_shift = g * all_shift + s
-            all_gain = g * all_gain
-            my_gain = jnp.where(p < q, all_gain, my_gain)
-            my_shift = jnp.where(p < q, all_shift, my_shift)
-        tot1_n = n
-        tot2[it, n, 0:1, :] = all_gain
-        tot2[it, n, 1:2, :] = all_shift
-        got2[it, n, y, 0:1, :] = all_gain
-        got2[it, n, y, 1:2, :] = all_shift
-        bnd_gain_shift[n, 0:1, :] = my_gain
-        bnd_gain_shift[n, 1:2, :] = my_shift
-
-        def send(j, carry):
-            stage2(it, n, j).start()
-            return carry
-
-        lax.fori_loop(1, LINES, send, 0)
-
-    bnd_gain_shift = diag.at[:, 3:5, :]
-
-    def entering_state(it, n):
-        def receive(j, carry):
-            source = lax.rem(y + j, LINES)
-            remote(tot2.at[it, n], got2.at[it, n, source], s2.at[it, n, j], r2.at[it, n, source], (tm, z)).wait_recv()
-            return carry
-
-        lax.fori_loop(1, LINES, receive, 0)
-        state = h0[:, pl.ds(pl.multiple_of(n * CW, CW), CW)]
-        for p in range(LINES - 1):
-            g, s = got2[it, n, p, 0:1, :], got2[it, n, p, 1:2, :]
-            state = jnp.where(p < y, g * state + s, state)
-        state = diag[n, 3:4, :] * state + diag[n, 4:5, :]
-        return eg[n] * state + es[n]
-
-    def loop(body):
+        def join(p, state):
+            return totals[it, p, 0:1, :] * state + totals[it, p, 1:2, :]
+
+        lax.fori_loop(0, tm, receive, 0)
+        mine[0:1, :] = lax.fori_loop(0, tm, join, h0[...])
+
+    def enter_of(n):
+        return eg[n] * mine[0:1, pl.ds(pl.multiple_of(n * CW, CW), CW)] + es[n]
+
+    def loop(body, first=0, end=NC):
         def step(n, carry):
             body(n)
             return carry
 
-        lax.fori_loop(0, NC, step, 0)
+        lax.fori_loop(first, end, step, 0)
 
     def apply_middle(n):
-        enter = entering_state(0, n)
+        enter = enter_of(n)
         hprev[n, 0:SUB, :] = enter
         xb[1, 0, n, 0:SUB, :] = enter.astype(jnp.bfloat16)
         for i in range(ROWS // SUB - 1):
@@ -277,7 +262,7 @@
         return pltpu.make_async_copy(outv.at[n], out.at[:, cols], out_sem.at[n])
 
     def apply_last(n):
-        enter = entering_state(1, n)
+        enter = enter_of(n)
         for i in range(ROWS // SUB):
             state = gs[n, tile_of(i), :] * enter + ss[n, tile_of(i), :]
             states[n, tile_of(i), :] = state.astype(jnp.bfloat16)
@@ -295,30 +280,47 @@
                     diag[n, g : g + 1, :] = jnp.sum(jnp.where(same, square, 0.0), axis=0, keepdims=True)
         accumulate(it, [(0, c) for c in range(NC)], True)
         for c in range(NC):
-            if it == 0 and c == 0:
-                load_weights(1).wait()
-                load_weights(3).wait()
-                edges[0].wait_recv()
-                edges[2].start()
-                edges[1].wait_recv()
-                edges[3].start()
-            left_c = (c + half) % NC
+            opposite = (c + half) % NC
             to_right(it, c).wait_recv()
-            to_left(it, left_c).wait_recv()
+            to_left(it, opposite).wait_recv()
             if c < half:
                 forward(it, c).start()
-                forward(it, left_c).start()
-            accumulate(it, [(3, c), (1, left_c)], False)
+                forward(it, opposite).start()
+            if c < half - 1:
+                continue
+            if c == half - 1:
+                if it == 0:
+                    edges[0].wait_recv()
+                    edges[2].start()
+                    edges[1].wait_recv()
+                    edges[3].start()
+                    hear(1, partner)
+                    tell(2, y_pair)
+                    load_weights(1).wait()
+                    load_weights(3).wait()
+                for k in range(half - 1):
+                    accumulate(it, [(3, k), (1, k + half)])
+            accumulate(it, [(3, c), (1, opposite)])
+            if it == 0 and c == half:
+                hear(2, y_pair)
+                tell(3, y_pair)
         if it == 0:
             load_weights(2).wait()
             edges[2].wait_recv()
             edges[3].wait_recv()
+            hear(3, y_pair)
         for c in range(half):
             forward(it, c).wait_recv()
             forward(it, c + half).wait_recv()
-            accumulate(it, [(2, c), (2, c + half)], False)
-        loop(functools.partial(gates, it))
-        loop(functools.partial(middle, it))
+            if c < half - 1:
+                accumulate(it, [(2, c), (2, c + half)])
+        for n in range(NC):
+            accumulate(it, [(2, half - 1), (2, NC - 1)], parts=[n])
+            if n > 0:
+                gates(it, n - 1)
+        gates(it, NC - 1)
+        send_totals(it)
+        enter_block(it)
         loop(apply_middle if it == 0 else apply_last)
 
     boundary.wait_send()
@@ -330,19 +332,13 @@
             to_left(it, c).wait_send()
             forward(it, c).wait_send()
 
-        def drain(n):
-            def one(j, carry):
-                stage1(it, n, j).wait_send()
-                return carry
-
-            def two(j, carry):
-                stage2(it, n, j).wait_send()
-                return carry
-
-            lax.fori_loop(1, GROUP, one, 0)
-            lax.fori_loop(1, LINES, two, 0)
-
-        loop(drain)
+        for away in AWAY:
+            device, copy = total_to(it, away)
+
+            @pl.when(device > tm)
+            def _():
+                copy.wait_send()
+
     loop(lambda n: store_out(n).wait())
 
 
@@ -370,10 +366,9 @@
             pltpu.VMEM((NC, SUB, CW), f32),
             pltpu.VMEM((NC, 8, CW), f32),
             pltpu.VMEM((SUB, UNITS), bf16),
-            pltpu.VMEM((ITERS, NC, 2, CW), f32),
-            pltpu.VMEM((ITERS, NC, 2, CW), f32),
-            pltpu.VMEM((ITERS, NC, GROUP, 2, CW), f32),
-            pltpu.VMEM((ITERS, NC, LINES, 2, CW), f32),
+            pltpu.VMEM((ITERS, 2, UNITS), f32),
+            pltpu.VMEM((ITERS, STEPS, 2, UNITS), f32),
+            pltpu.VMEM((8, UNITS), f32),
             pltpu.VMEM((2, ROWS, ROWS), bf16),
             pltpu.VMEM((NC, ROWS, CW), bf16),
             pltpu.VMEM((NC, ROWS, CW), bf16),
@@ -387,10 +382,9 @@
             dma((ITERS, 4, NC)),
             dma((4,)),
             dma((4,)),
-            dma((ITERS, NC, GROUP)),
-            dma((ITERS, NC, GROUP)),
-            dma((ITERS, NC, LINES)),
-            dma((ITERS, NC, LINES)),
+            dma((ITERS, STEPS)),
+            dma((ITERS, STEPS)),
+            pltpu.SemaphoreType.REGULAR((4,)),
         ],
         compiler_params=pltpu.CompilerParams(
             collective_id=0, has_side_effects=True, vmem_limit_bytes=58 * 2**20

time: 69.8 us -> 64.8 us (0.928)
  the two profiles are of different devices: /device:TPU:1 before, /device:TPU:25 now
where the time goes in v2:
time: 64.8 us; the launch traced here: 64.6 us
  Pallas kernels  62.7 us (97%)
  local copies, waits for them, and re-layouts  1.87 us (3%)
    pallas_call x1, Pallas kernels, per_device(): pl.pallas_call(kernel, out_shape=jax.ShapeDtypeStruct((ROWS, UNITS), bf16...  62.7 us
    unnamed x1, local copies, waits for them, and re-layouts  1.87 us

profile of v2, /device:TPU:25, one launch (start us, length us, event | category | flops | bytes accessed | tf_op | source)
XLA Modules:
  0.0 64.6 jit_solution(11927899164330237402)
XLA Ops:
  0.0 62.7 %shard_map.46 = bf16[256,1024]{1,0:T(8,128)(2,1)} custom-call(bf16[3,256,1024]{2,1,0:T(8,128)(2,1)} %bitcast.2, bf16[3,4096,1024]{2,1,0:T(8,128)(2,1)} %w.1, f32[1,1024]{1,0:T(1,128)} %bitcast.3, bf16[256,1024]{1,0:T(8,128)(2,1)} %guess.1), custom_call_target="tpu_custom_call" | custom-call | tf_op jit(solution)/shard_map/pallas_call | solution.py:350
  62.7 1.9 %copy.6 = bf16[256,1024]{1,0:T(8,128)(2,1)} copy(bf16[256,1024]{1,0:T(8,128)(2,1)} %shard_map.46) | data formatting | bytes 1048576

commit v3 on v2

v3 whole, which is shorter than its diff:
```python
import jax
import jax.numpy as jnp
from jax import lax
from jax.experimental import pallas as pl
from jax.experimental.pallas import tpu as pltpu
from jax.sharding import PartitionSpec as P

ITERS = 2
ROWS = 256
UNITS = 1024
SUB = 16
CW = 256
NC = UNITS // CW
GROUP = 8
LINES = 4
LANES = 128
ZC = UNITS // LANES
XS = 4
STEPS = GROUP * LINES
AWAY = sorted(
    [(a, b, c) for a in range(LINES) for b in range(XS) for c in range(2) if (a, b, c) != (0, 0, 0)],
    key=lambda k: -(min(k[0], LINES - k[0]) + min(k[1], XS - k[1])),
)
MESH = pl.DeviceIdType.MESH


def dot(a, b):
    return jnp.dot(a, b, preferred_element_type=jnp.float32)


def sigmoid(x):
    return 0.5 * jnp.tanh(0.5 * x) + 0.5


def kernel(
    gi, w, h0, guess, out,
    wv, giv, gv, xb, acc, ip, hprev, gs, ss, eg, es, diag, last, edge, top, total, totals, mine, perm, states, outv,
    load_sem, w_sem, out_sem, last_sem, right_s, left_s, fwd_s, z_r, edge_s, edge_r, t_s, t_r, known,
):
    tm = lax.axis_index("tm")
    z = lax.axis_index("hid")
    y, q = tm // GROUP, lax.rem(tm, GROUP)
    right, left = lax.rem(z + 1, 4), lax.rem(z + 3, 4)

    load_guess = pltpu.make_async_copy(guess, gv, load_sem.at[0])
    load_inputs = pltpu.make_async_copy(gi, giv, load_sem.at[1])

    def load_weights(d):
        rows = pl.ds(pl.multiple_of(lax.rem(z + d, 4) * UNITS, UNITS), UNITS)
        return pltpu.make_async_copy(w.at[:, rows, :], wv.at[d], w_sem.at[d])

    load_guess.start()
    load_weights(0).start()
    load_inputs.start()
    load_weights(1).start()
    load_weights(3).start()

    barrier = pltpu.get_barrier_semaphore()

    def greet(device):
        pl.semaphore_signal(barrier, inc=1, device_id=device, device_id_type=MESH)

    x, core = q // 2, lax.rem(q, 2)

    def device_at(a, b, c):
        return lax.rem(y + a, LINES) * GROUP + lax.rem(x + b, XS) * 2 + lax.rem(core + c, 2)

    x_pair = ((device_at(0, 1, 0), z), (device_at(0, XS - 1, 0), z))
    y_pair = ((device_at(1, 0, 0), z), (device_at(LINES - 1, 0, 0), z))
    partner = ((device_at(0, 0, 1), z),)
    later = (lax.rem(tm + 1, STEPS), z)
    earlier = (lax.rem(tm + STEPS - 1, STEPS), z)
    near = ((tm, right), (tm, left), later, earlier) + x_pair + y_pair + partner
    for device in near:
        greet(device)

    r = lax.broadcasted_iota(jnp.int32, (ROWS, ROWS), 0)
    t = lax.broadcasted_iota(jnp.int32, (ROWS, ROWS), 1)
    time = (r & (SUB - 1)) * SUB + (r >> 4)
    perm[0] = jnp.where(t == time, 1.0, 0.0).astype(jnp.bfloat16)
    perm[1] = jnp.where(t == time - 1, 1.0, 0.0).astype(jnp.bfloat16)

    load_guess.wait()

    last[0] = gv[ROWS - SUB :, :].astype(jnp.float32)[SUB - 1 :, :]
    for n in range(NC):
        rows = dot(perm[1], gv[:, n * CW : (n + 1) * CW])
        hprev[n] = rows
        for k in range(2):
            xb[0, 0, 2 * n + k] = rows[:, k * LANES : (k + 1) * LANES].astype(jnp.bfloat16)

    pl.semaphore_wait(barrier, len(near))

    def remote(src, dst, send, recv, device):
        return pltpu.make_async_remote_copy(
            src_ref=src, dst_ref=dst, send_sem=send, recv_sem=recv, device_id=device, device_id_type=MESH
        )

    half = NC // 2

    def part(it, d, m):
        return xb.at[it, d, pl.ds(2 * m, 2)]

    def to_right(it, m):
        return remote(part(it, 0, m), part(it, 3, m), right_s.at[it, m], z_r.at[it, 0, m], (tm, right))

    def to_left(it, m):
        return remote(part(it, 0, m), part(it, 1, m), left_s.at[it, m], z_r.at[it, 1, m], (tm, left))

    def forward(it, c, size):
        src, device = (3, right) if c < ZC // 2 else (1, left)
        here, there = xb.at[it, src, pl.ds(c, size)], xb.at[it, 2, pl.ds(c, size)]
        return remote(here, there, fwd_s.at[it, c], z_r.at[it, 2, c], (tm, device))

    boundary = remote(last.at[0], last.at[1], last_sem.at[0], last_sem.at[1], later)
    edges = (
        remote(edge.at[0], edge.at[3], edge_s.at[0], edge_r.at[0], (tm, right)),
        remote(edge.at[0], edge.at[1], edge_s.at[1], edge_r.at[1], (tm, left)),
        remote(edge.at[3], edge.at[2], edge_s.at[2], edge_r.at[2], (tm, right)),
    )

    boundary.start()
    for m in range(half):
        to_right(0, m).start()
        to_left(0, half + m).start()

    def tell(k, devices):
        for device in devices:
            pl.semaphore_signal(known.at[k], inc=1, device_id=device, device_id_type=MESH)

    def hear(k, devices):
        pl.semaphore_wait(known.at[k], len(devices))

    tell(0, x_pair)
    boundary.wait_recv()
    first = lax.broadcasted_iota(jnp.int32, (SUB, LANES), 0) == 0
    for c in range(ZC):
        cols = slice(c * LANES, (c + 1) * LANES)
        edge[0, :, cols] = jnp.where(tm == 0, h0[c : c + 1, :], last[1, :, cols])
    edges[0].start()
    edges[1].start()
    for m in range(half):
        to_right(0, half + m).start()
        to_left(0, m).start()
    for n in range(NC):
        for k in range(2):
            lanes = slice(k * LANES, (k + 1) * LANES)
            row = edge[0, :, n * CW + k * LANES : n * CW + (k + 1) * LANES]
            hprev[n, 0:SUB, lanes] = jnp.where(first, row, hprev[n, 0:SUB, lanes])

    def set_edge(d, pieces):
        for c in pieces:
            row = edge[d, :, c * LANES : (c + 1) * LANES]
            tile = xb[0, d, c, 0:SUB, :].astype(jnp.float32)
            top[d, c] = jnp.where(first, row, tile).astype(jnp.bfloat16)

    hear(0, x_pair)
    tell(1, partner)

    load_inputs.wait()

    for n in range(NC):
        for g in range(3):
            ip[n, g] = dot(perm[0], giv[g, :, n * CW : (n + 1) * CW])

    def block_piece(it, d, c):
        if it > 0:
            return xb[it, d, c]
        return jnp.concatenate([top[d, c], xb[it, d, c, SUB:, :]], axis=0)

    def accumulate(it, pieces, start=False, parts=range(NC)):
        for n in parts:
            cols = slice(n * CW, (n + 1) * CW)
            for g in range(3):
                terms = None if start else acc[n, g]
                for pair in zip(pieces[0::2], pieces[1::2]):
                    rows = jnp.concatenate([block_piece(it, d, c) for d, c in pair], axis=1)
                    (d0, c0), (d1, c1) = pair
                    if (d0, c0 + 1) == (d1, c1):
                        weights = wv[d0, g, c0 * LANES : (c0 + 2) * LANES, cols]
                    else:
                        weights = jnp.concatenate(
                            [wv[d, g, c * LANES : (c + 1) * LANES, cols] for d, c in pair], axis=0
                        )
                    term = dot(rows, weights)
                    terms = term if terms is None else terms + term
                acc[n, g] = terms

    sub_row = lax.broadcasted_iota(jnp.int32, (SUB, CW), 0)

    def tile_of(i):
        return slice(i * SUB, (i + 1) * SUB)

    def total_to(it, away):
        device = device_at(*away)
        copy = remote(total.at[it], totals.at[it, tm], t_s.at[it, device], t_r.at[it, tm], (device, z))
        return device, copy

    def total_from(it, p):
        return remote(total.at[it], totals.at[it, p], t_s.at[it, p], t_r.at[it, p], (tm, right))

    def gates(it, n):
        d0, d1, d2 = (jnp.broadcast_to(diag[n, g : g + 1, :], (SUB, CW)) for g in range(3))
        gain = shift_ = None
        for i in range(ROWS // SUB):
            rows = tile_of(i)
            previous = hprev[n, rows, :]
            memory = acc[n, 2, rows, :]
            update = sigmoid(ip[n, 0, rows, :] + acc[n, 0, rows, :])
            reset = sigmoid(ip[n, 1, rows, :] + acc[n, 1, rows, :])
            candidate = jnp.tanh(ip[n, 2, rows, :] + reset * memory)
            keep = 1.0 - update
            gap = previous - candidate
            target = candidate + update * gap
            slope = update + keep * (
                update * gap * d0
                + (1.0 - candidate * candidate) * reset * ((1.0 - reset) * memory * d1 + d2)
            )
            offset = target - slope * previous
            gain = slope if gain is None else slope * gain
            shift_ = offset if shift_ is None else slope * shift_ + offset
            gs[n, rows, :] = gain
            ss[n, rows, :] = shift_
        for k in (1, 2, 4, 8):
            before_gain = jnp.where(sub_row < k, 1.0, pltpu.roll(gain, k, 0))
            before_shift = jnp.where(sub_row < k, 0.0, pltpu.roll(shift_, k, 0))
            shift_ = gain * before_shift + shift_
            gain = gain * before_gain
        eg[n] = jnp.where(sub_row < 1, 1.0, pltpu.roll(gain, 1, 0))
        es[n] = jnp.where(sub_row < 1, 0.0, pltpu.roll(shift_, 1, 0))
        for k in range(2):
            lanes = slice(k * LANES, (k + 1) * LANES)
            row = slice(2 * n + k, 2 * n + k + 1)
            total[it, 0, row, :] = gain[SUB - 1 :, lanes]
            total[it, 1, row, :] = shift_[SUB - 1 :, lanes]

    def send_totals(it):
        for away in AWAY:
            device, copy = total_to(it, away)

            @pl.when(device > tm)
            def _():
                copy.start()

    def enter_block(it):
        def join(p, state):
            total_from(it, p).wait_recv()
            return totals[it, p, 0] * state + totals[it, p, 1]

        mine[...] = lax.fori_loop(0, tm, join, h0[...])

    def enter_of(n):
        row = jnp.concatenate([mine[2 * n : 2 * n + 1, :], mine[2 * n + 1 : 2 * n + 2, :]], axis=1)
        return eg[n] * row + es[n]

    def apply_middle(n):
        enter = enter_of(n)
        hprev[n, 0:SUB, :] = enter
        for k in range(2):
            lanes = slice(k * LANES, (k + 1) * LANES)
            xb[1, 0, 2 * n + k, 0:SUB, :] = enter[:, lanes].astype(jnp.bfloat16)
        for i in range(ROWS // SUB - 1):
            state = gs[n, tile_of(i), :] * enter + ss[n, tile_of(i), :]
            hprev[n, tile_of(i + 1), :] = state
            for k in range(2):
                lanes = slice(k * LANES, (k + 1) * LANES)
                xb[1, 0, 2 * n + k, tile_of(i + 1), :] = state[:, lanes].astype(jnp.bfloat16)
        to_right(1, n).start()
        to_left(1, n).start()

    def store_out(n):
        return pltpu.make_async_copy(outv.at[n], out.at[:, pl.ds(n * CW, CW)], out_sem.at[n])

    def apply_last(n):
        enter = enter_of(n)
        for i in range(ROWS // SUB):
            state = gs[n, tile_of(i), :] * enter + ss[n, tile_of(i), :]
            states[n, tile_of(i), :] = state.astype(jnp.bfloat16)
        outv[n] = dot(perm[0], states[n]).astype(jnp.bfloat16)
        store_out(n).start()

    for it in range(ITERS):
        if it == 0:
            load_weights(0).wait()
            same = r == t
            for n in range(NC):
                block = slice(n * CW, (n + 1) * CW)
                for g in range(3):
                    square = wv[0, g, block, block].astype(jnp.float32)
                    diag[n, g : g + 1, :] = jnp.sum(jnp.where(same, square, 0.0), axis=0, keepdims=True)
            set_edge(0, range(ZC))
        accumulate(it, [(0, c) for c in range(ZC)], True)
        for m in range(NC):
            opposite = (m + half) % NC
            to_right(it, m).wait_recv()
            to_left(it, opposite).wait_recv()
            if m == 0:
                forward(it, 0, 2).start()
                forward(it, 4, 2).start()
                if it == 0:
                    load_weights(2).start()
                continue
            fresh = [(3, 2 * m), (3, 2 * m + 1), (1, 2 * opposite), (1, 2 * opposite + 1)]
            if m == 1:
                if it == 0:
                    edges[0].wait_recv()
                    edges[2].start()
                for c in (2, 6, 3, 7):
                    forward(it, c, 1).start()
                fresh = [(3, 0), (3, 1), (1, 4), (1, 5)] + fresh
                if it == 0:
                    edges[1].wait_recv()
                    hear(1, partner)
                    tell(2, y_pair)
                    load_weights(1).wait()
                    load_weights(3).wait()
            if it == 0:
                for d, c in fresh:
                    set_edge(d, [c])
            accumulate(it, fresh)
            if it == 0 and m == half:
                hear(2, y_pair)
                tell(3, y_pair)
        if it == 0:
            load_weights(2).wait()
            edges[2].wait_recv()
            hear(3, y_pair)
        for c, size in ((0, 2), (2, 1), (3, 1)):
            forward(it, c, size).wait_recv()
            forward(it, c + ZC // 2, size).wait_recv()
            fresh = [(2, c + k) for k in range(size)] + [(2, c + ZC // 2 + k) for k in range(size)]
            if it == 0:
                for d, k in fresh:
                    set_edge(d, [k])
            if c < 3:
                accumulate(it, fresh)
        for n in range(NC):
            accumulate(it, fresh, parts=[n])
            if n > 0:
                gates(it, n - 1)
        gates(it, NC - 1)
        send_totals(it)
        enter_block(it)
        for n in range(NC):
            (apply_middle if it == 0 else apply_last)(n)

    boundary.wait_send()
    for copy in edges:
        copy.wait_send()
    for it in range(ITERS):
        for m in range(NC):
            to_right(it, m).wait_send()
            to_left(it, m).wait_send()
        for c, size in ((0, 2), (2, 1), (3, 1)):
            forward(it, c, size).wait_send()
            forward(it, c + ZC // 2, size).wait_send()
        for away in AWAY:
            device, copy = total_to(it, away)

            @pl.when(device > tm)
            def _():
                copy.wait_send()

    for n in range(NC):
        store_out(n).wait()


def per_device(gate_inputs, recurrent, initial_state, guess):
    bf16, f32 = jnp.bfloat16, jnp.float32
    dma = pltpu.SemaphoreType.DMA
    hbm = pl.BlockSpec(memory_space=pl.ANY)
    vmem = pl.BlockSpec(memory_space=pltpu.VMEM)
    return pl.pallas_call(
        kernel,
        out_shape=jax.ShapeDtypeStruct((ROWS, UNITS), bf16),
        in_specs=[hbm, hbm, vmem, hbm],
        out_specs=hbm,
        scratch_shapes=[
            pltpu.VMEM((4, 3, UNITS, UNITS), bf16),
            pltpu.VMEM((3, ROWS, UNITS), bf16),
            pltpu.VMEM((ROWS, UNITS), bf16),
            pltpu.VMEM((ITERS, 4, ZC, ROWS, LANES), bf16),
            pltpu.VMEM((NC, 3, ROWS, CW), f32),
            pltpu.VMEM((NC, 3, ROWS, CW), f32),
            pltpu.VMEM((NC, ROWS, CW), f32),
            pltpu.VMEM((NC, ROWS, CW), f32),
            pltpu.VMEM((NC, ROWS, CW), f32),
            pltpu.VMEM((NC, SUB, CW), f32),
            pltpu.VMEM((NC, SUB, CW), f32),
            pltpu.VMEM((NC, 8, CW), f32),
            pltpu.VMEM((2, 1, UNITS), f32),
            pltpu.VMEM((4, 1, UNITS), f32),
            pltpu.VMEM((4, ZC, SUB, LANES), bf16),
            pltpu.VMEM((ITERS, 2, 8, LANES), f32),
            pltpu.VMEM((ITERS, STEPS, 2, 8, LANES), f32),
            pltpu.VMEM((8, LANES), f32),
            pltpu.VMEM((2, ROWS, ROWS), bf16),
            pltpu.VMEM((NC, ROWS, CW), bf16),
            pltpu.VMEM((NC, ROWS, CW), bf16),
            dma((2,)),
            dma((4,)),
            dma((NC,)),
            dma((2,)),
            dma((ITERS, NC)),
            dma((ITERS, NC)),
            dma((ITERS, ZC)),
            dma((ITERS, 3, ZC)),
            dma((3,)),
            dma((3,)),
            dma((ITERS, STEPS)),
            dma((ITERS, STEPS)),
            pltpu.SemaphoreType.REGULAR((4,)),
        ],
        compiler_params=pltpu.CompilerParams(
            collective_id=0, has_side_effects=True, vmem_limit_bytes=58 * 2**20
        ),
    )(jnp.transpose(gate_inputs, (1, 0, 2)), recurrent, initial_state.reshape(8, LANES), guess)


def solution(mesh):
    in_specs = (P("tm", None, "hid"), P(None, None, "hid"), P("hid"), P("tm", "hid"))
    return jax.shard_map(
        per_device, mesh=mesh, in_specs=in_specs, out_specs=P("tm", "hid"), check_vma=False
    )
```

time: 64.8 us -> 61.8 us (0.954)
  Pallas kernels: 62.7 us -> 59.7 us
    pallas_call x1, Pallas kernels: 62.7 us -> 59.7 us  [per_device(): pl.pallas_call(kernel, out_shape=jax.ShapeDtypeStruct((ROWS, UNITS), bf16...]
where the time goes in v3:
time: 61.8 us; the launch traced here: 61.6 us
  Pallas kernels  59.7 us (97%)
  local copies, waits for them, and re-layouts  1.87 us (3%)
    pallas_call x1, Pallas kernels, per_device(): pl.pallas_call(kernel, out_shape=jax.ShapeDtypeStruct((ROWS, UNITS), bf16...  59.7 us
    unnamed x1, local copies, waits for them, and re-layouts  1.87 us

profile of v3, /device:TPU:25, one launch (start us, length us, event | category | flops | bytes accessed | tf_op | source)
XLA Modules:
  0.0 61.6 jit_solution(7011979208543346923)
XLA Ops:
  0.0 59.7 %shard_map.46 = bf16[256,1024]{1,0:T(8,128)(2,1)} custom-call(bf16[3,256,1024]{2,1,0:T(8,128)(2,1)} %bitcast.2, bf16[3,4096,1024]{2,1,0:T(8,128)(2,1)} %w.1, f32[8,128]{1,0:T(8,128)} %bitcast.3, bf16[256,1024]{1,0:T(8,128)(2,1)} %guess.1), custom_call_target="tpu_custom_call" | custom-call | tf_op jit(solution)/shard_map/pallas_call | solution.py:373
  59.7 1.9 %copy.6 = bf16[256,1024]{1,0:T(8,128)(2,1)} copy(bf16[256,1024]{1,0:T(8,128)(2,1)} %shard_map.46) | data formatting | bytes 1048576

commit v4 on v3

--- a/solution.py
+++ b/solution.py
@@ -34,8 +34,8 @@
 
 def kernel(
     gi, w, h0, guess, out,
-    wv, giv, gv, xb, acc, ip, hprev, gs, ss, eg, es, diag, last, edge, top, total, totals, mine, perm, states, outv,
-    load_sem, w_sem, out_sem, last_sem, right_s, left_s, fwd_s, z_r, edge_s, edge_r, t_s, t_r, known,
+    wv, giv, gv, xb, acc, ip, hprev, gs, ss, eg, es, diag, last, edge, top, total, totals, mine, perm, states, outv, terms_own, terms_got, enters,
+    load_sem, w_sem, out_sem, last_sem, right_s, left_s, fwd_s, z_r, edge_s, edge_r, t_s, t_r, known, terms_s, terms_r, enters_s, enters_r,
 ):
     tm = lax.axis_index("tm")
     z = lax.axis_index("hid")
@@ -118,6 +118,14 @@
         remote(edge.at[0], edge.at[1], edge_s.at[1], edge_r.at[1], (tm, left)),
         remote(edge.at[3], edge.at[2], edge_s.at[2], edge_r.at[2], (tm, right)),
     )
+
+    sides = ((tm, right), (tm, left))
+    terms_out = [
+        remote(terms_own, terms_got.at[k], terms_s.at[k], terms_r.at[k], sides[k]) for k in range(2)
+    ]
+    enters_out = [
+        remote(enters.at[2], enters.at[k], enters_s.at[k], enters_r.at[k], sides[k]) for k in range(2)
+    ]
 
     boundary.start()
     for m in range(half):
@@ -221,6 +229,11 @@
             shift_ = offset if shift_ is None else slope * shift_ + offset
             gs[n, rows, :] = gain
             ss[n, rows, :] = shift_
+            if it == 0 and n == 0 and i < ROWS // SUB - 1:
+                for k in range(2):
+                    lanes = slice(k * LANES, (k + 1) * LANES)
+                    terms_own[0, k, rows, :] = gain[:, lanes].astype(jnp.bfloat16)
+                    terms_own[1, k, rows, :] = shift_[:, lanes].astype(jnp.bfloat16)
         for k in (1, 2, 4, 8):
             before_gain = jnp.where(sub_row < k, 1.0, pltpu.roll(gain, k, 0))
             before_shift = jnp.where(sub_row < k, 0.0, pltpu.roll(shift_, k, 0))
@@ -265,8 +278,25 @@
             for k in range(2):
                 lanes = slice(k * LANES, (k + 1) * LANES)
                 xb[1, 0, 2 * n + k, tile_of(i + 1), :] = state[:, lanes].astype(jnp.bfloat16)
-        to_right(1, n).start()
-        to_left(1, n).start()
+        if n == 0:
+            for k in range(2):
+                enters[2, k] = enter[:, k * LANES : (k + 1) * LANES]
+            for copy in enters_out:
+                copy.start()
+        else:
+            to_right(1, n).start()
+            to_left(1, n).start()
+
+    def join_terms(k, d):
+        terms_out[k].wait_recv()
+        enters_out[k].wait_recv()
+        for j in range(2):
+            enter = enters[k, j]
+            xb[1, d, j, 0:SUB, :] = enter.astype(jnp.bfloat16)
+            for i in range(ROWS // SUB - 1):
+                gain = terms_got[k, 0, j, tile_of(i), :].astype(jnp.float32)
+                shift_ = terms_got[k, 1, j, tile_of(i), :].astype(jnp.float32)
+                xb[1, d, j, tile_of(i + 1), :] = (gain * enter + shift_).astype(jnp.bfloat16)
 
     def store_out(n):
         return pltpu.make_async_copy(outv.at[n], out.at[:, pl.ds(n * CW, CW)], out_sem.at[n])
@@ -290,7 +320,24 @@
                     diag[n, g : g + 1, :] = jnp.sum(jnp.where(same, square, 0.0), axis=0, keepdims=True)
             set_edge(0, range(ZC))
         accumulate(it, [(0, c) for c in range(ZC)], True)
-        for m in range(NC):
+        if it == 1:
+            join_terms(0, 3)
+            forward(it, 0, 2).start()
+            join_terms(1, 1)
+            accumulate(it, [(3, 0), (3, 1), (1, 0), (1, 1)])
+            for m in range(1, NC):
+                to_right(it, m).wait_recv()
+                to_left(it, m).wait_recv()
+                if m == 1:
+                    forward(it, 2, 1).start()
+                    forward(it, 3, 1).start()
+                elif m == 2:
+                    forward(it, 4, 2).start()
+                else:
+                    forward(it, 6, 1).start()
+                    forward(it, 7, 1).start()
+                accumulate(it, [(d, 2 * m + k) for d in (3, 1) for k in range(2)])
+        for m in range(NC if it == 0 else 0):
             opposite = (m + half) % NC
             to_right(it, m).wait_recv()
             to_left(it, opposite).wait_recv()
@@ -338,6 +385,9 @@
             accumulate(it, fresh, parts=[n])
             if n > 0:
                 gates(it, n - 1)
+            if it == 0 and n == 1:
+                for copy in terms_out:
+                    copy.start()
         gates(it, NC - 1)
         send_totals(it)
         enter_block(it)
@@ -345,10 +395,12 @@
             (apply_middle if it == 0 else apply_last)(n)
 
     boundary.wait_send()
+    for copy in terms_out + enters_out:
+        copy.wait_send()
     for copy in edges:
         copy.wait_send()
     for it in range(ITERS):
-        for m in range(NC):
+        for m in range(it, NC):
             to_right(it, m).wait_send()
             to_left(it, m).wait_send()
         for c, size in ((0, 2), (2, 1), (3, 1)):
@@ -397,6 +449,9 @@
             pltpu.VMEM((2, ROWS, ROWS), bf16),
             pltpu.VMEM((NC, ROWS, CW), bf16),
             pltpu.VMEM((NC, ROWS, CW), bf16),
+            pltpu.VMEM((2, 2, ROWS - SUB, LANES), bf16),
+            pltpu.VMEM((2, 2, 2, ROWS - SUB, LANES), bf16),
+            pltpu.VMEM((3, 2, SUB, LANES), f32),
             dma((2,)),
             dma((4,)),
             dma((NC,)),
@@ -410,6 +465,10 @@
             dma((ITERS, STEPS)),
             dma((ITERS, STEPS)),
             pltpu.SemaphoreType.REGULAR((4,)),
+            dma((2,)),
+            dma((2,)),
+            dma((2,)),
+            dma((2,)),
         ],
         compiler_params=pltpu.CompilerParams(
             collective_id=0, has_side_effects=True, vmem_limit_bytes=58 * 2**20

time: 61.8 us -> 58.9 us (0.953)
  Pallas kernels: 59.7 us -> 56.9 us
    pallas_call x1, Pallas kernels: 59.7 us -> 56.9 us  [per_device(): pl.pallas_call(kernel, out_shape=jax.ShapeDtypeStruct((ROWS, UNITS), bf16...]
where the time goes in v4:
time: 58.9 us; the launch traced here: 58.8 us
  Pallas kernels  56.9 us (97%)
  local copies, waits for them, and re-layouts  1.87 us (3%)
    pallas_call x1, Pallas kernels, per_device(): pl.pallas_call(kernel, out_shape=jax.ShapeDtypeStruct((ROWS, UNITS), bf16...  56.9 us
    unnamed x1, local copies, waits for them, and re-layouts  1.87 us

profile of v4, /device:TPU:25, one launch (start us, length us, event | category | flops | bytes accessed | tf_op | source)
XLA Modules:
  0.0 58.8 jit_solution(5113883228296479167)
XLA Ops:
  0.0 56.9 %shard_map.46 = bf16[256,1024]{1,0:T(8,128)(2,1)} custom-call(bf16[3,256,1024]{2,1,0:T(8,128)(2,1)} %bitcast.2, bf16[3,4096,1024]{2,1,0:T(8,128)(2,1)} %w.1, f32[8,128]{1,0:T(8,128)} %bitcast.3, bf16[256,1024]{1,0:T(8,128)(2,1)} %guess.1), custom_call_target="tpu_custom_call" | custom-call | tf_op jit(solution)/shard_map/pallas_call | solution.py:425
  56.9 1.9 %copy.6 = bf16[256,1024]{1,0:T(8,128)(2,1)} copy(bf16[256,1024]{1,0:T(8,128)(2,1)} %shard_map.46) | data formatting | bytes 1048576

commit v5 on v4

--- a/solution.py
+++ b/solution.py
@@ -34,8 +34,8 @@
 
 def kernel(
     gi, w, h0, guess, out,
-    wv, giv, gv, xb, acc, ip, hprev, gs, ss, eg, es, diag, last, edge, top, total, totals, mine, perm, states, outv, terms_own, terms_got, enters,
-    load_sem, w_sem, out_sem, last_sem, right_s, left_s, fwd_s, z_r, edge_s, edge_r, t_s, t_r, known, terms_s, terms_r, enters_s, enters_r,
+    wv, giv, gv, xb, acc, ip, hprev, gs, ss, eg, es, diag, last, edge, top, total, totals, mine, perm, states, terms_own, terms_got, enters,
+    load_sem, w_sem, last_sem, right_s, left_s, fwd_s, z_r, edge_s, edge_r, t_s, t_r, known, terms_s, terms_r, enters_s, enters_r,
 ):
     tm = lax.axis_index("tm")
     z = lax.axis_index("hid")
@@ -298,16 +298,12 @@
                 shift_ = terms_got[k, 1, j, tile_of(i), :].astype(jnp.float32)
                 xb[1, d, j, tile_of(i + 1), :] = (gain * enter + shift_).astype(jnp.bfloat16)
 
-    def store_out(n):
-        return pltpu.make_async_copy(outv.at[n], out.at[:, pl.ds(n * CW, CW)], out_sem.at[n])
-
     def apply_last(n):
         enter = enter_of(n)
         for i in range(ROWS // SUB):
             state = gs[n, tile_of(i), :] * enter + ss[n, tile_of(i), :]
             states[n, tile_of(i), :] = state.astype(jnp.bfloat16)
-        outv[n] = dot(perm[0], states[n]).astype(jnp.bfloat16)
-        store_out(n).start()
+        out[:, n * CW : (n + 1) * CW] = dot(perm[0], states[n]).astype(jnp.bfloat16)
 
     for it in range(ITERS):
         if it == 0:
@@ -413,9 +409,6 @@
             def _():
                 copy.wait_send()
 
-    for n in range(NC):
-        store_out(n).wait()
-
 
 def per_device(gate_inputs, recurrent, initial_state, guess):
     bf16, f32 = jnp.bfloat16, jnp.float32
@@ -426,7 +419,7 @@
         kernel,
         out_shape=jax.ShapeDtypeStruct((ROWS, UNITS), bf16),
         in_specs=[hbm, hbm, vmem, hbm],
-        out_specs=hbm,
+        out_specs=vmem,
         scratch_shapes=[
             pltpu.VMEM((4, 3, UNITS, UNITS), bf16),
             pltpu.VMEM((3, ROWS, UNITS), bf16),
@@ -448,13 +441,11 @@
             pltpu.VMEM((8, LANES), f32),
             pltpu.VMEM((2, ROWS, ROWS), bf16),
             pltpu.VMEM((NC, ROWS, CW), bf16),
-            pltpu.VMEM((NC, ROWS, CW), bf16),
             pltpu.VMEM((2, 2, ROWS - SUB, LANES), bf16),
             pltpu.VMEM((2, 2, 2, ROWS - SUB, LANES), bf16),
             pltpu.VMEM((3, 2, SUB, LANES), f32),
             dma((2,)),
             dma((4,)),
-            dma((NC,)),
             dma((2,)),
             dma((ITERS, NC)),
             dma((ITERS, NC)),
@@ -471,7 +462,7 @@
             dma((2,)),
         ],
         compiler_params=pltpu.CompilerParams(
-            collective_id=0, has_side_effects=True, vmem_limit_bytes=58 * 2**20
+            collective_id=0, has_side_effects=True, vmem_limit_bytes=53 * 2**20
         ),
     )(jnp.transpose(gate_inputs, (1, 0, 2)), recurrent, initial_state.reshape(8, LANES), guess)
 

time: 58.9 us -> 57.7 us (0.980)
  Pallas kernels: 56.9 us -> 56 us
    pallas_call x1, Pallas kernels: 56.9 us -> 56 us  [per_device(): pl.pallas_call(kernel, out_shape=jax.ShapeDtypeStruct((ROWS, UNITS), bf16...]
    unnamed x1 -> x3, local copies, waits for them, and re-layouts: 1.87 us -> 1.48 us
where the time goes in v5:
time: 57.7 us; the launch traced here: 57.5 us
  Pallas kernels  56 us (97%)
  local copies, waits for them, and re-layouts  1.48 us (3%)
    pallas_call x1, Pallas kernels, per_device(): pl.pallas_call(kernel, out_shape=jax.ShapeDtypeStruct((ROWS, UNITS), bf16...  56 us
    unnamed x3, local copies, waits for them, and re-layouts  1.48 us

profile of v5, /device:TPU:25, one launch (start us, length us, event | category | flops | bytes accessed | tf_op | source)
XLA Modules:
  0.0 57.5 jit_solution(17429681719250813778)
XLA Ops:
  0.0 0.0 copy-start
  0.0 0.7 %copy-done = f32[1024]{0:T(1024)S(1)} copy-done((f32[1024]{0:T(1024)S(1)}, f32[1024]{0:T(1024)}, u32[]{:S(2)}) %copy-start) | copy-done | bytes 4120
  0.7 56.0 %shard_map.46 = bf16[256,1024]{1,0:T(8,128)(2,1)S(1)} custom-call(bf16[3,256,1024]{2,1,0:T(8,128)(2,1)} %bitcast.3, bf16[3,4096,1024]{2,1,0:T(8,128)(2,1)} %w.1, f32[8,128]{1,0:T(8,128)S(1)} %bitcast.2, bf16[256,1024]{1,0:T(8,128)(2,1)} %guess.1), custom_call_target="tpu_custom_call" | custom-call | tf_op jit(solution)/shard_map/pallas_call | solution.py:418
  56.7 0.8 %copy.6 = bf16[256,1024]{1,0:T(8,128)(2,1)} copy(bf16[256,1024]{1,0:T(8,128)(2,1)S(1)} %shard_map.46) | data formatting | bytes 1048576
Async XLA Ops:
  0.0 0.7 %copy-start = (f32[1024]{0:T(1024)S(1)}, f32[1024]{0:T(1024)}, u32[]{:S(2)}) copy-start(f32[1024]{0:T(1024)} %param.6) | copy-start | bytes 12292

commit v6 on v5

--- a/solution.py
+++ b/solution.py
@@ -305,6 +305,27 @@
             states[n, tile_of(i), :] = state.astype(jnp.bfloat16)
         out[:, n * CW : (n + 1) * CW] = dot(perm[0], states[n]).astype(jnp.bfloat16)
 
+    def drain(it):
+        if it == 0:
+            boundary.wait_send()
+            for copy in edges:
+                copy.wait_send()
+        else:
+            for copy in terms_out + enters_out:
+                copy.wait_send()
+        for m in range(it, NC):
+            to_right(it, m).wait_send()
+            to_left(it, m).wait_send()
+        for c, size in ((0, 2), (2, 1), (3, 1)):
+            forward(it, c, size).wait_send()
+            forward(it, c + ZC // 2, size).wait_send()
+        for away in AWAY:
+            device, copy = total_to(it, away)
+
+            @pl.when(device > tm)
+            def _():
+                copy.wait_send()
+
     for it in range(ITERS):
         if it == 0:
             load_weights(0).wait()
@@ -320,6 +341,7 @@
             join_terms(0, 3)
             forward(it, 0, 2).start()
             join_terms(1, 1)
+            drain(0)
             accumulate(it, [(3, 0), (3, 1), (1, 0), (1, 1)])
             for m in range(1, NC):
                 to_right(it, m).wait_recv()
@@ -390,24 +412,7 @@
         for n in range(NC):
             (apply_middle if it == 0 else apply_last)(n)
 
-    boundary.wait_send()
-    for copy in terms_out + enters_out:
-        copy.wait_send()
-    for copy in edges:
-        copy.wait_send()
-    for it in range(ITERS):
-        for m in range(it, NC):
-            to_right(it, m).wait_send()
-            to_left(it, m).wait_send()
-        for c, size in ((0, 2), (2, 1), (3, 1)):
-            forward(it, c, size).wait_send()
-            forward(it, c + ZC // 2, size).wait_send()
-        for away in AWAY:
-            device, copy = total_to(it, away)
-
-            @pl.when(device > tm)
-            def _():
-                copy.wait_send()
+    drain(1)
 
 
 def per_device(gate_inputs, recurrent, initial_state, guess):

time: 57.7 us -> 57.6 us (level)
  no operation moved by 1% of the time
where the time goes in v6:
time: 57.6 us; the launch traced here: 57.5 us
  Pallas kernels  56 us (97%)
  local copies, waits for them, and re-layouts  1.48 us (3%)
    pallas_call x1, Pallas kernels, per_device(): pl.pallas_call(kernel, out_shape=jax.ShapeDtypeStruct((ROWS, UNITS), bf16...  56 us
    unnamed x3, local copies, waits for them, and re-layouts  1.48 us

profile of v6, /device:TPU:25, one launch (start us, length us, event | category | flops | bytes accessed | tf_op | source)
XLA Modules:
  0.0 57.5 jit_solution(17823311018179488251)
XLA Ops:
  0.0 0.0 copy-start
  0.0 0.7 %copy-done = f32[1024]{0:T(1024)S(1)} copy-done((f32[1024]{0:T(1024)S(1)}, f32[1024]{0:T(1024)}, u32[]{:S(2)}) %copy-start) | copy-done | bytes 4120
  0.7 56.0 %shard_map.46 = bf16[256,1024]{1,0:T(8,128)(2,1)S(1)} custom-call(bf16[3,256,1024]{2,1,0:T(8,128)(2,1)} %bitcast.3, bf16[3,4096,1024]{2,1,0:T(8,128)(2,1)} %w.1, f32[8,128]{1,0:T(8,128)S(1)} %bitcast.2, bf16[256,1024]{1,0:T(8,128)(2,1)} %guess.1), custom_call_target="tpu_custom_call" | custom-call | tf_op jit(solution)/shard_map/pallas_call | solution.py:423
  56.7 0.8 %copy.6 = bf16[256,1024]{1,0:T(8,128)(2,1)} copy(bf16[256,1024]{1,0:T(8,128)(2,1)S(1)} %shard_map.46) | data formatting | bytes 1048576
Async XLA Ops:
  0.0 0.7 %copy-start = (f32[1024]{0:T(1024)S(1)}, f32[1024]{0:T(1024)}, u32[]{:S(2)}) copy-start(f32[1024]{0:T(1024)} %param.6) | copy-start | bytes 12292
